TPU v7x, 512 devices: a whole 4x4x16 slice. The times are simulated.
512 devices in a mesh: dom: 64 (over x, z), orb: 8 (over y, core).
Axes of the slice: x: 4, y: 4, z: 16, core: 2. Of those that a mesh axis runs over, the one named last changes fastest.
Arguments:
- orbitals: bfloat16 [3072, 64, 512], P('dom', 'orb'), may hold values from -6 to 6
- adjoint_source: bfloat16 [3072, 64, 512], P('dom', 'orb'), may hold values from -6 to 6
- eigenvalues: float32 [64], P('orb'), may hold values from -1 to -0.25
- cell_scale: float32 [3072], P('dom'), may hold values from 0.4 to 1.6
- base_potential: float32 [3072, 512], P('dom'), may hold values from 0.5 to 1.5
- stiffness: bfloat16 [512, 512], replicated, may hold values from -1.5 to 1.5, as said below
- face_perm: int32 [3072, 64], P('dom'), may hold values from 0 to 63, each once within a row
- restrict: bfloat16 [512, 64], replicated, may hold values from -0.25 to 0.25
- prolong: bfloat16 [64, 512], replicated, may hold values from -0.75 to 0.75
- owner: int32 [3072, 1], P('dom'), may hold values from 0 to 63; in each aligned block of 48 rows (0 to 47, 48 to 95, ...) at most 2 rows name the same one
- pot_slot: int32 [3072], P('dom'), may hold values from 0 to 63
- potential: float32 [4096, 64], P('dom'), may hold values from -6 to 6
Outputs:
- adjoint: bfloat16 [3072, 64, 512], P('dom', 'orb')
- updated: float32 [4096, 64], P('dom')
- applied: bfloat16 [3072, 64, 512], P('dom', 'orb')
Inputs may be any that keep to these rules, and one draw needn't show every extreme that they name: In the rows of one device no owner is named by more than 2 cells. `face_perm`: each row is a permutation. `stiffness`: symmetric.
All inputs are finite; a program needn't handle non-finite values.
Results may differ from a plain program's by a relative error of at most 0.0027.
Values sent between devices are 32-bit elements; how exact they have to be, the bound alone decides.
No kernel may reach another device: no remote copies, remote signals or barrier semaphores. Data moves between devices by JAX's collectives and lax.ppermute only.
A program may use at most 64 MiB of HBM per device.

v0:
```python
import jax
import jax.numpy as jnp
from jax import lax
from jax.sharding import PartitionSpec as P

ITERS = 4
relax = 0.25
step_rate = 0.1


def padded_2(block, sides, width):
    for axis, dim in sides:
        count = lax.axis_size(axis)
        forward = [(i, i + 1) for i in range(count - 1)]
        backward = [(target, source) for source, target in forward]
        low = lax.ppermute(
            lax.slice_in_dim(block, block.shape[dim] - width, None, axis=dim), axis, forward
        )
        high = lax.ppermute(lax.slice_in_dim(block, 0, width, axis=dim), axis, backward)
        block = jnp.concatenate([low, block, high], axis=dim)
    return block


def local(
    orbitals,
    adjoint_source,
    eigenvalues,
    cell_scale,
    base_potential,
    stiffness,
    face_perm,
    restrict,
    prolong,
    owner,
    pot_slot,
    potential,
):
    nodes = stiffness.shape[0]
    faces = face_perm.shape[1]
    pot_rows = potential.shape[0]
    n_domains = lax.axis_size("dom")
    cell_count = owner.shape[0]
    capacity = 2 * ((cell_count + n_domains - 1) // n_domains)
    onehot = (face_perm[:, :, None] == jnp.arange(faces, dtype=jnp.int32)[None, None, :]).astype(
        jnp.float32
    )

    def assemble_local(partial_sum):
        left_face = partial_sum[:, :, :faces]
        right_face = partial_sum[:, :, nodes - faces :]
        sent_right = jnp.einsum("ckj,cok->coj", onehot, right_face, precision=lax.Precision.HIGHEST)
        boundary = jnp.stack([left_face[0], sent_right[-1]], 0)
        padded = padded_2(boundary, (("dom", 0),), 1)
        left_next = jnp.concatenate([left_face[1:], padded[3][None]], 0)
        add_right = jnp.einsum("ckj,coj->cok", onehot, left_next, precision=lax.Precision.HIGHEST)
        add_left = jnp.concatenate([padded[0][None], sent_right[:-1]], 0)
        return jnp.concatenate(
            [
                left_face + add_left,
                partial_sum[:, :, faces : nodes - faces],
                right_face + add_right,
            ],
            2,
        )

    def operator(values_bf, values_full, shift):
        kinetic = jnp.dot(
            values_bf.reshape(-1, nodes), stiffness, preferred_element_type=jnp.float32
        ).reshape(values_full.shape)
        return assemble_local(cell_scale[:, None, None] * kinetic + shift * values_full)

    source = adjoint_source.astype(jnp.float32)
    shift = base_potential[:, None, :] - eigenvalues[None, :, None]
    iterate = relax * source
    for step_index in range(ITERS):
        image = operator(iterate.astype(jnp.bfloat16), iterate, shift)
        iterate = iterate + relax * (source - image)
    adjoint = iterate.astype(jnp.bfloat16)
    partial_density = jnp.sum(orbitals.astype(jnp.float32) * iterate, axis=1)
    restrict_full = restrict.astype(jnp.float32)
    density_term = lax.psum(partial_density, "orb")
    projected = jnp.dot(density_term, restrict_full, precision=lax.Precision.HIGHEST)
    coarse_cols = projected.shape[1]
    dest_owner = owner[:, 0]
    owner_hot = (dest_owner[:, None] == jnp.arange(n_domains, dtype=jnp.int32)[None, :]).astype(
        jnp.int32
    )
    earlier = jnp.cumsum(owner_hot, axis=0) - owner_hot
    rank_within = jnp.sum(earlier * owner_hot, axis=1)
    slot_index = dest_owner * capacity + rank_within
    send_hot_int = (
        slot_index[None, :] == jnp.arange(n_domains * capacity, dtype=jnp.int32)[:, None]
    ).astype(jnp.int32)
    send_hot = send_hot_int.astype(jnp.float32)
    send_values = jnp.dot(send_hot, projected, precision=lax.Precision.HIGHEST).reshape(
        n_domains, capacity, coarse_cols
    )
    send_ids = (jnp.sum(send_hot_int * (pot_slot + 1)[None, :], axis=1) - 1).reshape(
        n_domains, capacity
    )
    recv_values, recv_ids = (
        lax.all_to_all(send_values, "dom", split_axis=0, concat_axis=0, tiled=True),
        lax.all_to_all(send_ids, "dom", split_axis=0, concat_axis=0, tiled=True),
    )
    recv_hot = (
        recv_ids.reshape(-1)[None, :] == jnp.arange(pot_rows, dtype=jnp.int32)[:, None]
    ).astype(jnp.float32)
    summed = jnp.dot(
        recv_hot, recv_values.reshape(-1, coarse_cols), precision=lax.Precision.HIGHEST
    )
    updated = potential - step_rate * summed
    every_pot = lax.all_gather(updated, "dom", axis=0, tiled=True)
    cell_pot = every_pot[dest_owner * pot_rows + pot_slot]
    node_potential = jnp.dot(cell_pot, prolong.astype(jnp.float32), precision=lax.Precision.HIGHEST)
    shift_new = (base_potential + node_potential)[:, None, :]
    applied = operator(orbitals, orbitals.astype(jnp.float32), shift_new).astype(jnp.bfloat16)
    return (adjoint, updated, applied)


def solution(mesh):
    in_specs = (
        P("dom", "orb", None),
        P("dom", "orb", None),
        P("orb"),
        P("dom"),
        P("dom", None),
        P(),
        P("dom", None),
        P(),
        P(),
        P("dom", None),
        P("dom"),
        P("dom", None),
    )
    out_specs = (P("dom", "orb", None), P("dom", None), P("dom", "orb", None))
    return jax.shard_map(local, mesh=mesh, in_specs=in_specs, out_specs=out_specs, check_vma=False)
```

profile of v0, /device:TPU:2, one launch (start us, length us, event | category | flops | bytes accessed | tf_op | source)
XLA Modules:
  0.0 320.8 jit_solution(6365384118985894531)
XLA Ops:
  7.2 0.0 all-reduce.2.cloned.1.call-start
  7.3 1.0 copy-done
  8.2 1.6 fusion.10
  9.8 11.4 %collective-permute-start.1 = (f32[1,8,64]{2,1,0:T(8,128)S(1)}, f32[1,8,64]{2,1,0:T(8,128)S(1)}, u32[]{:S(2)}, u32[]{:S(2)}) collective-permute-start(f32[1,8,64]{2,1,0:T(8,128)S(1)} %slice.159), channel_id=1, source_target_pairs={{8,0},{16,8},{24,16},{32,24},{40,32},{48,40},{56,48},{64,56},{72,6... | collective-permute-start | bytes 6152 | tf_op jit(solution)/shard_map/ppermute | solution.py:19
  21.2 1.4 fusion.9
  22.7 1.9 collective-permute-start
  24.6 0.1 fusion.77
  24.7 0.1 reduce_window_sum.11
  24.7 0.2 select_reduce_fusion.1
  24.9 0.1 select_reduce_fusion
  25.1 0.2 slice.157
  25.4 1.4 fusion.15
  26.8 3.5 %collective-permute-done = f32[1,8,64]{2,1,0:T(8,128)S(1)} collective-permute-done((f32[1,8,64]{2,1,0:T(8,128)S(1)}, f32[1,8,64]{2,1,0:T(8,128)S(1)}, u32[]{:S(2)}, u32[]{:S(2)}) %collective-permute-start) | collective-permute-done | bytes 2080 | tf_op jit(solution)/shard_map/ppermute | solution.py:16
  30.3 0.8 fusion.11
  31.2 2.6 collective-permute-start.3
  33.8 1.4 fusion.7
  35.3 0.2 slice.164
  35.5 3.3 %collective-permute-start.2 = (f32[1,8,64]{2,1,0:T(8,128)S(1)}, f32[1,8,64]{2,1,0:T(8,128)S(1)}, u32[]{:S(2)}, u32[]{:S(2)}) collective-permute-start(f32[1,8,64]{2,1,0:T(8,128)S(1)} %slice.162), channel_id=1, source_target_pairs={{0,8},{8,16},{16,24},{24,32},{32,40},{40,48},{48,56},{56,64},{64,7... | collective-permute-start | bytes 6152 | tf_op jit(solution)/shard_map/ppermute | solution.py:16
  38.8 1.4 fusion.16
  40.2 2.9 collective-permute-done.2
  43.2 0.6 fusion.27
  43.8 0.4 fusion.12
  44.2 1.9 collective-permute-start.5
  46.1 1.4 fusion.5
  47.6 0.2 slice.171
  47.8 3.9 %collective-permute-start.4 = (f32[1,8,64]{2,1,0:T(8,128)S(1)}, f32[1,8,64]{2,1,0:T(8,128)S(1)}, u32[]{:S(2)}, u32[]{:S(2)}) collective-permute-start(f32[1,8,64]{2,1,0:T(8,128)S(1)} %slice.169), channel_id=1, source_target_pairs={{0,8},{8,16},{16,24},{24,32},{32,40},{40,48},{48,56},{56,64},{64,7... | collective-permute-start | bytes 6152 | tf_op jit(solution)/shard_map/ppermute | solution.py:16
  51.8 1.4 fusion.17
  53.2 2.3 collective-permute-done.4
  55.5 0.8 fusion.13
  56.3 1.9 collective-permute-start.7
  58.3 1.4 fusion.3
  59.8 0.2 slice.178
  60.0 3.9 %collective-permute-start.6 = (f32[1,8,64]{2,1,0:T(8,128)S(1)}, f32[1,8,64]{2,1,0:T(8,128)S(1)}, u32[]{:S(2)}, u32[]{:S(2)}) collective-permute-start(f32[1,8,64]{2,1,0:T(8,128)S(1)} %slice.176), channel_id=1, source_target_pairs={{0,8},{8,16},{16,24},{24,32},{32,40},{40,48},{48,56},{56,64},{64,7... | collective-permute-start | bytes 6152 | tf_op jit(solution)/shard_map/ppermute | solution.py:16
  63.9 1.4 fusion.18
  65.3 2.3 collective-permute-done.6
  67.7 2.1 fusion.24
  69.8 0.0 all-reduce.2.cloned.1.call-update
  69.8 0.8 sub.46
  70.5 5.7 %all-to-all-start = ((s32[64,1,2]{2,1,0:T(1,128)}), s32[64,1,2]{2,1,0:T(1,128)S(1)}, u32[]{:S(2)}, u32[]{:S(2)}) async-start(s32[64,1,2]{2,1,0:T(1,128)} %bitcast.2), calls=%async_computation | async-start | bytes 65536 | tf_op jit(solution)/shard_map/all_to_all | solution.py:103
  76.3 58.1 %all-reduce.2.cloned.1.call-done = f32[48,512]{1,0:T(8,128)} async-done(((f32[48,512]{1,0:T(8,128)}), f32[48,512]{1,0:T(8,128)}) %all-reduce.2.cloned.1.call-update) | async-done | bytes 98320 | tf_op jit(solution)/shard_map/psum | solution.py:81
  134.3 1.1 fusion.90
  135.4 0.3 fusion.74
  135.8 0.7 reshape.85
  136.5 15.9 %all-to-all-start.1 = ((f32[64,1,128]{2,1,0:T(1,128)}), f32[64,1,128]{2,1,0:T(1,128)S(1)}, u32[]{:S(2)}, u32[]{:S(2)}) async-start(f32[64,1,128]{2,1,0:T(1,128)} %reshape.85), calls=%async_computation.1 | async-start | bytes 65536 | tf_op jit(solution)/shard_map/all_to_all | solution.py:102
  152.4 0.0 all-gather.2.cloned.1.call-start
  152.5 0.5 broadcast.70
  153.0 0.7 reduce.3
  153.7 0.1 eq.63
  153.8 12.0 %all-to-all-done.1 = f32[64,1,128]{2,1,0:T(1,128)S(1)} async-done(((f32[64,1,128]{2,1,0:T(1,128)}), f32[64,1,128]{2,1,0:T(1,128)S(1)}, u32[]{:S(2)}, u32[]{:S(2)}) %all-to-all-start.1) | async-done | bytes 32800 | tf_op jit(solution)/shard_map/all_to_all | solution.py:102
  165.9 0.5 broadcast.72
  166.4 0.7 reduce.4
  167.1 0.1 reshape.86
  167.2 0.8 fusion.21
  168.0 128.1 %all-gather.2.cloned.1.call-done = f32[4096,64]{1,0:T(8,128)} async-done(((f32[64,64]{1,0:T(8,128)}), f32[4096,64]{1,0:T(8,128)}) %all-gather.2.cloned.1.call-update) | async-done | bytes 1048592 | tf_op jit(solution)/shard_map/all_gather | solution.py:112
  296.1 2.2 gather_fusion
  298.3 0.2 convolution_add_fusion
  298.5 0.4 fusion.14
  298.9 4.8 %collective-permute-start.9 = (f32[1,8,64]{2,1,0:T(8,128)S(1)}, f32[1,8,64]{2,1,0:T(8,128)S(1)}, u32[]{:S(2)}, u32[]{:S(2)}) collective-permute-start(f32[1,8,64]{2,1,0:T(8,128)S(1)} %slice.187), channel_id=1, source_target_pairs={{8,0},{16,8},{24,16},{32,24},{40,32},{48,40},{56,48},{64,56},{72,6... | collective-permute-start | bytes 6152 | tf_op jit(solution)/shard_map/ppermute | solution.py:19
  303.7 1.4 fusion.1
  305.2 0.1 slice.211
  305.4 1.9 collective-permute-start.8
  307.3 1.6 fusion.20
  308.9 4.1 %collective-permute-done.8 = f32[1,8,64]{2,1,0:T(8,128)S(1)} collective-permute-done((f32[1,8,64]{2,1,0:T(8,128)S(1)}, f32[1,8,64]{2,1,0:T(8,128)S(1)}, u32[]{:S(2)}, u32[]{:S(2)}) %collective-permute-start.8) | collective-permute-done | bytes 2080 | tf_op jit(solution)/shard_map/ppermute | solution.py:16
  313.0 1.0 pad_maximum_fusion
  (58 shorter events, 0.6 us)
Async XLA Ops:
  7.2 1.0 copy-start
  7.2 14.0 %copy-start.11 = (s32[48,64]{1,0:T(8,128)S(1)}, s32[48,64]{1,0:T(8,128)}, u32[]{:S(2)}) copy-start(s32[48,64]{1,0:T(8,128)} %param.18) | copy-start | bytes 36868
  7.2 17.4 %copy-start.7 = (s32[48,1]{0,1:T(1,128)S(1)}, s32[48,1]{0,1:T(1,128)}, u32[]{:S(2)}) copy-start(s32[48,1]{0,1:T(1,128)} %param.21) | copy-start | bytes 580
  7.2 17.7 %copy-start.9 = (s32[48]{0:T(128)S(1)}, s32[48]{0:T(128)}, u32[]{:S(2)}) copy-start(s32[48]{0:T(128)} %param.22) | copy-start | bytes 580
  7.2 127.1 %all-reduce.2.cloned.1.call-start = ((), (), s32[]{:S(2)}) async-start(), calls=%async_computation.2 | async-start | bytes 196608 | tf_op jit(solution)/shard_map/psum | solution.py:81
  9.8 15.5 %collective-permute-start.1 = (f32[1,8,64]{2,1,0:T(8,128)S(1)}, f32[1,8,64]{2,1,0:T(8,128)S(1)}, u32[]{:S(2)}, u32[]{:S(2)}) collective-permute-start(f32[1,8,64]{2,1,0:T(8,128)S(1)} %slice.159), channel_id=1, source_target_pairs={{8,0},{16,8},{24,16},{32,24},{40,32},{48,40},{56,48},{64,56},{72,6... | collective-permute-start | bytes 6152 | tf_op jit(solution)/shard_map/ppermute | solution.py:19
  22.7 7.6 %collective-permute-start = (f32[1,8,64]{2,1,0:T(8,128)S(1)}, f32[1,8,64]{2,1,0:T(8,128)S(1)}, u32[]{:S(2)}, u32[]{:S(2)}) collective-permute-start(f32[1,8,64]{2,1,0:T(8,128)S(1)} %slice.155), channel_id=1, source_target_pairs={{0,8},{8,16},{16,24},{24,32},{32,40},{40,48},{48,56},{56,64},{64,7... | collective-permute-start | bytes 6152 | tf_op jit(solution)/shard_map/ppermute | solution.py:16
  25.0 5.3 %copy-start.1 = (bf16[48,8,512]{2,1,0:T(8,128)(2,1)S(1)}, bf16[48,8,512]{2,1,0:T(8,128)(2,1)}, u32[]{:S(2)}) copy-start(bf16[48,8,512]{2,1,0:T(8,128)(2,1)} %param.13) | copy-start | bytes 1179652
  25.1 5.3 %copy-start.3 = (f32[48,512]{1,0:T(8,128)S(1)}, f32[48,512]{1,0:T(8,128)}, u32[]{:S(2)}) copy-start(f32[48,512]{1,0:T(8,128)} %param.16) | copy-start | bytes 294916
  25.1 5.3 %copy-start.8 = (f32[48]{0:T(128)S(1)}, f32[48]{0:T(128)}, u32[]{:S(2)}) copy-start(f32[48]{0:T(128)} %param.15) | copy-start | bytes 580
  25.1 5.3 %copy-start.10 = (f32[8]{0:T(128)S(1)}, f32[8]{0:T(128)}, u32[]{:S(2)}) copy-start(f32[8]{0:T(128)} %param.14) | copy-start | bytes 100
  31.2 7.6 %collective-permute-start.3 = (f32[1,8,64]{2,1,0:T(8,128)S(1)}, f32[1,8,64]{2,1,0:T(8,128)S(1)}, u32[]{:S(2)}, u32[]{:S(2)}) collective-permute-start(f32[1,8,64]{2,1,0:T(8,128)S(1)} %slice.166), channel_id=1, source_target_pairs={{8,0},{16,8},{24,16},{32,24},{40,32},{48,40},{56,48},{64,56},{72,6... | collective-permute-start | bytes 6152 | tf_op jit(solution)/shard_map/ppermute | solution.py:19
  35.5 7.6 %collective-permute-start.2 = (f32[1,8,64]{2,1,0:T(8,128)S(1)}, f32[1,8,64]{2,1,0:T(8,128)S(1)}, u32[]{:S(2)}, u32[]{:S(2)}) collective-permute-start(f32[1,8,64]{2,1,0:T(8,128)S(1)} %slice.162), channel_id=1, source_target_pairs={{0,8},{8,16},{16,24},{24,32},{32,40},{40,48},{48,56},{56,64},{64,7... | collective-permute-start | bytes 6152 | tf_op jit(solution)/shard_map/ppermute | solution.py:16
  44.2 7.6 %collective-permute-start.5 = (f32[1,8,64]{2,1,0:T(8,128)S(1)}, f32[1,8,64]{2,1,0:T(8,128)S(1)}, u32[]{:S(2)}, u32[]{:S(2)}) collective-permute-start(f32[1,8,64]{2,1,0:T(8,128)S(1)} %slice.173), channel_id=1, source_target_pairs={{8,0},{16,8},{24,16},{32,24},{40,32},{48,40},{56,48},{64,56},{72,6... | collective-permute-start | bytes 6152 | tf_op jit(solution)/shard_map/ppermute | solution.py:19
  47.8 7.6 %collective-permute-start.4 = (f32[1,8,64]{2,1,0:T(8,128)S(1)}, f32[1,8,64]{2,1,0:T(8,128)S(1)}, u32[]{:S(2)}, u32[]{:S(2)}) collective-permute-start(f32[1,8,64]{2,1,0:T(8,128)S(1)} %slice.169), channel_id=1, source_target_pairs={{0,8},{8,16},{16,24},{24,32},{32,40},{40,48},{48,56},{56,64},{64,7... | collective-permute-start | bytes 6152 | tf_op jit(solution)/shard_map/ppermute | solution.py:16
  56.3 7.6 %collective-permute-start.7 = (f32[1,8,64]{2,1,0:T(8,128)S(1)}, f32[1,8,64]{2,1,0:T(8,128)S(1)}, u32[]{:S(2)}, u32[]{:S(2)}) collective-permute-start(f32[1,8,64]{2,1,0:T(8,128)S(1)} %slice.180), channel_id=1, source_target_pairs={{8,0},{16,8},{24,16},{32,24},{40,32},{48,40},{56,48},{64,56},{72,6... | collective-permute-start | bytes 6152 | tf_op jit(solution)/shard_map/ppermute | solution.py:19
  59.7 8.0 %copy-start.2 = (bf16[48,8,512]{2,1,0:T(8,128)(2,1)S(1)}, bf16[48,8,512]{2,1,0:T(8,128)(2,1)}, u32[]{:S(2)}) copy-start(bf16[48,8,512]{2,1,0:T(8,128)(2,1)} %param.12) | copy-start | bytes 1179652
  60.0 7.6 %collective-permute-start.6 = (f32[1,8,64]{2,1,0:T(8,128)S(1)}, f32[1,8,64]{2,1,0:T(8,128)S(1)}, u32[]{:S(2)}, u32[]{:S(2)}) collective-permute-start(f32[1,8,64]{2,1,0:T(8,128)S(1)} %slice.176), channel_id=1, source_target_pairs={{0,8},{8,16},{16,24},{24,32},{32,40},{40,48},{48,56},{56,64},{64,7... | collective-permute-start | bytes 6152 | tf_op jit(solution)/shard_map/ppermute | solution.py:16
  67.6 66.7 %copy-start.4 = (bf16[512,64]{0,1:T(8,128)(2,1)S(1)}, bf16[512,64]{0,1:T(8,128)(2,1)}, u32[]{:S(2)}) copy-start(bf16[512,64]{0,1:T(8,128)(2,1)} %param.19) | copy-start | bytes 196612
  67.7 99.5 %copy-start.6 = (f32[64,64]{1,0:T(8,128)S(1)}, f32[64,64]{1,0:T(8,128)}, u32[]{:S(2)}) copy-start(f32[64,64]{1,0:T(8,128)} %param.23) | copy-start | bytes 49156
  67.7 230.6 %copy-start.5 = (bf16[64,512]{1,0:T(8,128)(2,1)S(1)}, bf16[64,512]{1,0:T(8,128)(2,1)}, u32[]{:S(2)}) copy-start(bf16[64,512]{1,0:T(8,128)(2,1)} %param.20) | copy-start | bytes 196612
  70.5 65.9 %all-to-all-start = ((s32[64,1,2]{2,1,0:T(1,128)}), s32[64,1,2]{2,1,0:T(1,128)S(1)}, u32[]{:S(2)}, u32[]{:S(2)}) async-start(s32[64,1,2]{2,1,0:T(1,128)} %bitcast.2), calls=%async_computation | async-start | bytes 65536 | tf_op jit(solution)/shard_map/all_to_all | solution.py:103
  136.5 29.4 %all-to-all-start.1 = ((f32[64,1,128]{2,1,0:T(1,128)}), f32[64,1,128]{2,1,0:T(1,128)S(1)}, u32[]{:S(2)}, u32[]{:S(2)}) async-start(f32[64,1,128]{2,1,0:T(1,128)} %reshape.85), calls=%async_computation.1 | async-start | bytes 65536 | tf_op jit(solution)/shard_map/all_to_all | solution.py:102
  152.4 143.7 %all-gather.2.cloned.1.call-start = ((), (), s32[]{:S(2)}) async-start(), calls=%async_computation.3 | async-start | bytes 2129920 | tf_op jit(solution)/shard_map/all_gather | solution.py:112
  298.9 8.4 %collective-permute-start.9 = (f32[1,8,64]{2,1,0:T(8,128)S(1)}, f32[1,8,64]{2,1,0:T(8,128)S(1)}, u32[]{:S(2)}, u32[]{:S(2)}) collective-permute-start(f32[1,8,64]{2,1,0:T(8,128)S(1)} %slice.187), channel_id=1, source_target_pairs={{8,0},{16,8},{24,16},{32,24},{40,32},{48,40},{56,48},{64,56},{72,6... | collective-permute-start | bytes 6152 | tf_op jit(solution)/shard_map/ppermute | solution.py:19
  305.4 7.6 %collective-permute-start.8 = (f32[1,8,64]{2,1,0:T(8,128)S(1)}, f32[1,8,64]{2,1,0:T(8,128)S(1)}, u32[]{:S(2)}, u32[]{:S(2)}) collective-permute-start(f32[1,8,64]{2,1,0:T(8,128)S(1)} %slice.183), channel_id=1, source_target_pairs={{0,8},{8,16},{16,24},{24,32},{32,40},{40,48},{48,56},{56,64},{64,7... | collective-permute-start | bytes 6152 | tf_op jit(solution)/shard_map/ppermute | solution.py:16
Sparse Core Ops, SparseCore 0:
  69.9 64.3 all-reduce.1
  168.1 127.9 all-gather.1
where the time goes:
time: 321 us
  waiting for transfers between devices  213 us (66%)
  starting transfers between devices  59.2 us (18%)
  matrix products  20.7 us (6%)
  between operations  14.7 us (5%)
  local copies, waits for them, and re-layouts  7.21 us (2%)
  other arithmetic  5.72 us (2%)
    all_gather x1, waiting for transfers between devices, local(): every_pot = lax.all_gather(updated, 'dom', axis=0, tiled=True)  128 us
    psum x1, waiting for transfers between devices, local(): density_term = lax.psum(partial_density, 'orb')  58.1 us
    ppermute x5, starting transfers between devices, padded_2(): lax.ppermute(lax.slice_in_dim(block, 0, width, axis=dim), axis, backward)  22.6 us
    all_to_all x1, starting transfers between devices, local(): lax.all_to_all(send_values, 'dom', split_axis=0, concat_axis=0, tiled=True)  15.9 us
    ppermute x5, waiting for transfers between devices, padded_2(): lax.ppermute(lax.slice_in_dim(block, block.shape[dim] - width, None, axis...  15 us
    ppermute x5, starting transfers between devices, padded_2(): lax.ppermute(lax.slice_in_dim(block, block.shape[dim] - width, None, axis...  15 us
    all_to_all x1, waiting for transfers between devices, local(): lax.all_to_all(send_values, 'dom', split_axis=0, concat_axis=0, tiled=True)  12 us
    dot_general x5, matrix products, assemble_local(): jnp.einsum('ckj,coj->cok', onehot, left_next, precision=lax.Precision.HIG...  7.2 us
  transfers between devices with their start and end apart: 14, of which 8 were waited for; matrix products, arithmetic and copies ran while one was open for 6% of the time, Pallas kernels for 0%

commit v1 on v0

--- a/solution.py
+++ b/solution.py
@@ -109,7 +109,9 @@
         recv_hot, recv_values.reshape(-1, coarse_cols), precision=lax.Precision.HIGHEST
     )
     updated = potential - step_rate * summed
-    every_pot = lax.all_gather(updated, "dom", axis=0, tiled=True)
+    every_pot = jnp.concatenate(
+        lax.all_to_all(jnp.stack([updated] * lax.axis_size("dom")), "dom", 0, 0), axis=0
+    )
     cell_pot = every_pot[dest_owner * pot_rows + pot_slot]
     node_potential = jnp.dot(cell_pot, prolong.astype(jnp.float32), precision=lax.Precision.HIGHEST)
     shift_new = (base_potential + node_potential)[:, None, :]

time: 321 us -> 253 us (0.79)
  the two profiles are of different devices: /device:TPU:2 before, /device:TPU:30 now
where the time goes in v1:
time: 253 us
  waiting for transfers between devices  132 us (52%)
  starting transfers between devices  65.2 us (26%)
  matrix products  20.1 us (8%)
  between operations  14.7 us (6%)
  local copies, waits for them, and re-layouts  11.9 us (5%)
  other arithmetic  8.99 us (4%)
    psum x1, waiting for transfers between devices, local(): density_term = lax.psum(partial_density, 'orb')  55.3 us
    all_to_all x1, waiting for transfers between devices, local(): lax.all_to_all(jnp.stack([updated] * lax.axis_size('dom')), 'dom', 0, 0)  52.5 us
    ppermute x5, starting transfers between devices, padded_2(): lax.ppermute(lax.slice_in_dim(block, 0, width, axis=dim), axis, backward)  20 us
    ppermute x5, starting transfers between devices, padded_2(): lax.ppermute(lax.slice_in_dim(block, block.shape[dim] - width, None, axis...  17 us
    all_to_all x1, starting transfers between devices, local(): lax.all_to_all(send_values, 'dom', split_axis=0, concat_axis=0, tiled=True)  16.1 us
    ppermute x5, waiting for transfers between devices, padded_2(): lax.ppermute(lax.slice_in_dim(block, block.shape[dim] - width, None, axis...  13 us
    all_to_all x1, waiting for transfers between devices, local(): lax.all_to_all(send_values, 'dom', split_axis=0, concat_axis=0, tiled=True)  11.1 us
    dot_general x5, matrix products, assemble_local(): jnp.einsum('ckj,coj->cok', onehot, left_next, precision=lax.Precision.HIG...  7.2 us
  transfers between devices with their start and end apart: 14, of which 8 were waited for; matrix products, arithmetic and copies ran while one was open for 8% of the time, Pallas kernels for 0%

profile of v1, /device:TPU:30, one launch (start us, length us, event | category | flops | bytes accessed | tf_op | source)
XLA Modules:
  0.0 252.7 jit_solution(2680980851029094778)
XLA Ops:
  7.3 1.0 copy-done
  8.2 1.6 fusion.10
  9.8 11.7 %collective-permute-start.1 = (f32[1,8,64]{2,1,0:T(8,128)S(1)}, f32[1,8,64]{2,1,0:T(8,128)S(1)}, u32[]{:S(2)}, u32[]{:S(2)}) collective-permute-start(f32[1,8,64]{2,1,0:T(8,128)S(1)} %slice.159), channel_id=1, source_target_pairs={{8,0},{16,8},{24,16},{32,24},{40,32},{48,40},{56,48},{64,56},{72,6... | collective-permute-start | bytes 6152 | tf_op jit(solution)/shard_map/ppermute | solution.py:19
  21.5 1.4 fusion.9
  22.9 1.9 collective-permute-start
  25.0 0.2 select_reduce_fusion.1
  25.2 0.1 select_reduce_fusion
  25.4 0.2 slice.157
  25.7 1.4 fusion.15
  27.1 3.5 %collective-permute-done = f32[1,8,64]{2,1,0:T(8,128)S(1)} collective-permute-done((f32[1,8,64]{2,1,0:T(8,128)S(1)}, f32[1,8,64]{2,1,0:T(8,128)S(1)}, u32[]{:S(2)}, u32[]{:S(2)}) %collective-permute-start) | collective-permute-done | bytes 2080 | tf_op jit(solution)/shard_map/ppermute | solution.py:16
  30.6 0.8 fusion.11
  31.5 2.6 %collective-permute-start.3 = (f32[1,8,64]{2,1,0:T(8,128)S(1)}, f32[1,8,64]{2,1,0:T(8,128)S(1)}, u32[]{:S(2)}, u32[]{:S(2)}) collective-permute-start(f32[1,8,64]{2,1,0:T(8,128)S(1)} %slice.166), channel_id=1, source_target_pairs={{8,0},{16,8},{24,16},{32,24},{40,32},{48,40},{56,48},{64,56},{72,6... | collective-permute-start | bytes 6152 | tf_op jit(solution)/shard_map/ppermute | solution.py:19
  34.1 1.4 fusion.7
  35.6 0.2 slice.164
  35.8 3.3 %collective-permute-start.2 = (f32[1,8,64]{2,1,0:T(8,128)S(1)}, f32[1,8,64]{2,1,0:T(8,128)S(1)}, u32[]{:S(2)}, u32[]{:S(2)}) collective-permute-start(f32[1,8,64]{2,1,0:T(8,128)S(1)} %slice.162), channel_id=1, source_target_pairs={{0,8},{8,16},{16,24},{24,32},{32,40},{40,48},{48,56},{56,64},{64,7... | collective-permute-start | bytes 6152 | tf_op jit(solution)/shard_map/ppermute | solution.py:16
  39.1 1.4 fusion.16
  40.5 2.9 %collective-permute-done.2 = f32[1,8,64]{2,1,0:T(8,128)S(1)} collective-permute-done((f32[1,8,64]{2,1,0:T(8,128)S(1)}, f32[1,8,64]{2,1,0:T(8,128)S(1)}, u32[]{:S(2)}, u32[]{:S(2)}) %collective-permute-start.2) | collective-permute-done | bytes 2080 | tf_op jit(solution)/shard_map/ppermute | solution.py:16
  43.5 0.6 fusion.27
  44.1 0.4 fusion.12
  44.5 1.9 collective-permute-start.5
  46.4 1.4 fusion.5
  47.9 0.2 slice.171
  48.1 3.9 %collective-permute-start.4 = (f32[1,8,64]{2,1,0:T(8,128)S(1)}, f32[1,8,64]{2,1,0:T(8,128)S(1)}, u32[]{:S(2)}, u32[]{:S(2)}) collective-permute-start(f32[1,8,64]{2,1,0:T(8,128)S(1)} %slice.169), channel_id=1, source_target_pairs={{0,8},{8,16},{16,24},{24,32},{32,40},{40,48},{48,56},{56,64},{64,7... | collective-permute-start | bytes 6152 | tf_op jit(solution)/shard_map/ppermute | solution.py:16
  52.1 1.4 fusion.17
  53.5 2.3 collective-permute-done.4
  55.8 0.8 fusion.13
  56.6 1.9 collective-permute-start.7
  58.5 1.4 fusion.3
  60.0 0.2 slice.178
  60.3 3.9 %collective-permute-start.6 = (f32[1,8,64]{2,1,0:T(8,128)S(1)}, f32[1,8,64]{2,1,0:T(8,128)S(1)}, u32[]{:S(2)}, u32[]{:S(2)}) collective-permute-start(f32[1,8,64]{2,1,0:T(8,128)S(1)} %slice.176), channel_id=1, source_target_pairs={{0,8},{8,16},{16,24},{24,32},{32,40},{40,48},{48,56},{56,64},{64,7... | collective-permute-start | bytes 6152 | tf_op jit(solution)/shard_map/ppermute | solution.py:16
  64.2 1.4 fusion.18
  65.6 2.3 collective-permute-done.6
  68.0 2.1 fusion.24
  70.1 0.7 sub.46
  70.8 5.5 %all-to-all-start = ((s32[64,1,2]{2,1,0:T(1,128)}), s32[64,1,2]{2,1,0:T(1,128)S(1)}, u32[]{:S(2)}, u32[]{:S(2)}) async-start(s32[64,1,2]{2,1,0:T(1,128)} %bitcast.2), calls=%async_computation | async-start | bytes 65536 | tf_op jit(solution)/shard_map/all_to_all | solution.py:103
  76.4 55.3 %all-reduce.2.cloned.1.call-done = f32[48,512]{1,0:T(8,128)} async-done(((f32[48,512]{1,0:T(8,128)}), f32[48,512]{1,0:T(8,128)}) %all-reduce.2.cloned.1.call-update) | async-done | bytes 98320 | tf_op jit(solution)/shard_map/psum | solution.py:81
  131.7 1.1 fusion.90
  132.8 0.3 fusion.74
  133.1 0.7 reshape.91
  133.8 16.1 %all-to-all-start.1 = ((f32[64,1,128]{2,1,0:T(1,128)}), f32[64,1,128]{2,1,0:T(1,128)S(1)}, u32[]{:S(2)}, u32[]{:S(2)}) async-start(f32[64,1,128]{2,1,0:T(1,128)} %reshape.91), calls=%async_computation.1 | async-start | bytes 65536 | tf_op jit(solution)/shard_map/all_to_all | solution.py:102
  149.9 0.5 broadcast.72
  150.5 0.7 reduce.3
  151.2 0.1 eq.63
  151.3 11.1 %all-to-all-done.1 = f32[64,1,128]{2,1,0:T(1,128)S(1)} async-done(((f32[64,1,128]{2,1,0:T(1,128)}), f32[64,1,128]{2,1,0:T(1,128)S(1)}, u32[]{:S(2)}, u32[]{:S(2)}) %all-to-all-start.1) | async-done | bytes 32800 | tf_op jit(solution)/shard_map/all_to_all | solution.py:102
  162.4 0.5 broadcast.74
  162.9 0.7 reduce.4
  163.7 0.1 reshape.92
  163.8 0.2 fusion.21
  164.0 0.2 stack.2
  164.2 2.3 reshape.93
  166.5 6.5 %all-to-all-start.2 = ((f32[64,1,4096]{2,1,0:T(1,128)}), f32[64,1,4096]{2,1,0:T(1,128)S(1)}, u32[]{:S(2)}, u32[]{:S(2)}) async-start(f32[64,1,4096]{2,1,0:T(1,128)} %reshape.93), calls=%async_computation.2 | async-start | bytes 2097152 | tf_op jit(solution)/shard_map/all_to_all | solution.py:113
  173.0 52.5 %all-to-all-done.2 = f32[64,1,4096]{2,1,0:T(1,128)S(1)} async-done(((f32[64,1,4096]{2,1,0:T(1,128)}), f32[64,1,4096]{2,1,0:T(1,128)S(1)}, u32[]{:S(2)}, u32[]{:S(2)}) %all-to-all-start.2) | async-done | bytes 1048608 | tf_op jit(solution)/shard_map/all_to_all | solution.py:113
  225.5 3.3 %reduce.5 = f32[64,4096]{1,0:T(8,128)S(1)} reduce(f32[64,1,4096]{2,1,0:T(1,128)S(1)} %all-to-all-done.2, f32[]{:T(128)} %broadcast.74), dimensions={1}, to_apply=%all_to_all.12.reduce_sub_computation | reduce | bytes 2097156 | tf_op jit(solution)/shard_map/all_to_all | solution.py:113
  228.8 2.2 reshape.94
  230.9 2.2 gather_fusion
  233.1 0.2 convolution_add_fusion
  233.3 0.4 fusion.14
  233.7 1.9 collective-permute-start.9
  235.6 1.4 fusion.1
  237.1 0.1 slice.211
  237.3 3.9 %collective-permute-start.8 = (f32[1,8,64]{2,1,0:T(8,128)S(1)}, f32[1,8,64]{2,1,0:T(8,128)S(1)}, u32[]{:S(2)}, u32[]{:S(2)}) collective-permute-start(f32[1,8,64]{2,1,0:T(8,128)S(1)} %slice.183), channel_id=1, source_target_pairs={{0,8},{8,16},{16,24},{24,32},{32,40},{40,48},{48,56},{56,64},{64,7... | collective-permute-start | bytes 6152 | tf_op jit(solution)/shard_map/ppermute | solution.py:16
  241.2 1.6 fusion.20
  242.8 2.1 collective-permute-done.8
  244.9 1.0 pad_maximum_fusion
  (63 shorter events, 0.8 us)
Async XLA Ops:
  7.2 1.0 copy-start
  7.2 14.3 %copy-start.12 = (s32[48,64]{1,0:T(8,128)S(1)}, s32[48,64]{1,0:T(8,128)}, u32[]{:S(2)}) copy-start(s32[48,64]{1,0:T(8,128)} %param.18) | copy-start | bytes 36868
  7.2 17.7 %copy-start.8 = (s32[48,1]{0,1:T(1,128)S(1)}, s32[48,1]{0,1:T(1,128)}, u32[]{:S(2)}) copy-start(s32[48,1]{0,1:T(1,128)} %param.21) | copy-start | bytes 580
  7.2 18.0 %copy-start.10 = (s32[48]{0:T(128)S(1)}, s32[48]{0:T(128)}, u32[]{:S(2)}) copy-start(s32[48]{0:T(128)} %param.22) | copy-start | bytes 580
  7.2 124.5 %all-reduce.2.cloned.1.call-start = ((), (), s32[]{:S(2)}) async-start(), calls=%async_computation.3 | async-start | bytes 196608 | tf_op jit(solution)/shard_map/psum | solution.py:81
  9.8 15.8 %collective-permute-start.1 = (f32[1,8,64]{2,1,0:T(8,128)S(1)}, f32[1,8,64]{2,1,0:T(8,128)S(1)}, u32[]{:S(2)}, u32[]{:S(2)}) collective-permute-start(f32[1,8,64]{2,1,0:T(8,128)S(1)} %slice.159), channel_id=1, source_target_pairs={{8,0},{16,8},{24,16},{32,24},{40,32},{48,40},{56,48},{64,56},{72,6... | collective-permute-start | bytes 6152 | tf_op jit(solution)/shard_map/ppermute | solution.py:19
  22.9 7.6 %collective-permute-start = (f32[1,8,64]{2,1,0:T(8,128)S(1)}, f32[1,8,64]{2,1,0:T(8,128)S(1)}, u32[]{:S(2)}, u32[]{:S(2)}) collective-permute-start(f32[1,8,64]{2,1,0:T(8,128)S(1)} %slice.155), channel_id=1, source_target_pairs={{0,8},{8,16},{16,24},{24,32},{32,40},{40,48},{48,56},{56,64},{64,7... | collective-permute-start | bytes 6152 | tf_op jit(solution)/shard_map/ppermute | solution.py:16
  25.3 5.3 %copy-start.1 = (bf16[48,8,512]{2,1,0:T(8,128)(2,1)S(1)}, bf16[48,8,512]{2,1,0:T(8,128)(2,1)}, u32[]{:S(2)}) copy-start(bf16[48,8,512]{2,1,0:T(8,128)(2,1)} %param.13) | copy-start | bytes 1179652
  25.3 5.3 %copy-start.3 = (f32[48,512]{1,0:T(8,128)S(1)}, f32[48,512]{1,0:T(8,128)}, u32[]{:S(2)}) copy-start(f32[48,512]{1,0:T(8,128)} %param.16) | copy-start | bytes 294916
  25.4 5.3 %copy-start.9 = (f32[48]{0:T(128)S(1)}, f32[48]{0:T(128)}, u32[]{:S(2)}) copy-start(f32[48]{0:T(128)} %param.15) | copy-start | bytes 580
  25.4 5.3 %copy-start.11 = (f32[8]{0:T(128)S(1)}, f32[8]{0:T(128)}, u32[]{:S(2)}) copy-start(f32[8]{0:T(128)} %param.14) | copy-start | bytes 100
  31.5 7.6 %collective-permute-start.3 = (f32[1,8,64]{2,1,0:T(8,128)S(1)}, f32[1,8,64]{2,1,0:T(8,128)S(1)}, u32[]{:S(2)}, u32[]{:S(2)}) collective-permute-start(f32[1,8,64]{2,1,0:T(8,128)S(1)} %slice.166), channel_id=1, source_target_pairs={{8,0},{16,8},{24,16},{32,24},{40,32},{48,40},{56,48},{64,56},{72,6... | collective-permute-start | bytes 6152 | tf_op jit(solution)/shard_map/ppermute | solution.py:19
  35.8 7.6 %collective-permute-start.2 = (f32[1,8,64]{2,1,0:T(8,128)S(1)}, f32[1,8,64]{2,1,0:T(8,128)S(1)}, u32[]{:S(2)}, u32[]{:S(2)}) collective-permute-start(f32[1,8,64]{2,1,0:T(8,128)S(1)} %slice.162), channel_id=1, source_target_pairs={{0,8},{8,16},{16,24},{24,32},{32,40},{40,48},{48,56},{56,64},{64,7... | collective-permute-start | bytes 6152 | tf_op jit(solution)/shard_map/ppermute | solution.py:16
  44.5 7.6 %collective-permute-start.5 = (f32[1,8,64]{2,1,0:T(8,128)S(1)}, f32[1,8,64]{2,1,0:T(8,128)S(1)}, u32[]{:S(2)}, u32[]{:S(2)}) collective-permute-start(f32[1,8,64]{2,1,0:T(8,128)S(1)} %slice.173), channel_id=1, source_target_pairs={{8,0},{16,8},{24,16},{32,24},{40,32},{48,40},{56,48},{64,56},{72,6... | collective-permute-start | bytes 6152 | tf_op jit(solution)/shard_map/ppermute | solution.py:19
  48.1 7.6 %collective-permute-start.4 = (f32[1,8,64]{2,1,0:T(8,128)S(1)}, f32[1,8,64]{2,1,0:T(8,128)S(1)}, u32[]{:S(2)}, u32[]{:S(2)}) collective-permute-start(f32[1,8,64]{2,1,0:T(8,128)S(1)} %slice.169), channel_id=1, source_target_pairs={{0,8},{8,16},{16,24},{24,32},{32,40},{40,48},{48,56},{56,64},{64,7... | collective-permute-start | bytes 6152 | tf_op jit(solution)/shard_map/ppermute | solution.py:16
  56.6 7.6 %collective-permute-start.7 = (f32[1,8,64]{2,1,0:T(8,128)S(1)}, f32[1,8,64]{2,1,0:T(8,128)S(1)}, u32[]{:S(2)}, u32[]{:S(2)}) collective-permute-start(f32[1,8,64]{2,1,0:T(8,128)S(1)} %slice.180), channel_id=1, source_target_pairs={{8,0},{16,8},{24,16},{32,24},{40,32},{48,40},{56,48},{64,56},{72,6... | collective-permute-start | bytes 6152 | tf_op jit(solution)/shard_map/ppermute | solution.py:19
  60.0 8.0 %copy-start.2 = (bf16[48,8,512]{2,1,0:T(8,128)(2,1)S(1)}, bf16[48,8,512]{2,1,0:T(8,128)(2,1)}, u32[]{:S(2)}) copy-start(bf16[48,8,512]{2,1,0:T(8,128)(2,1)} %param.12) | copy-start | bytes 1179652
  60.3 7.6 %collective-permute-start.6 = (f32[1,8,64]{2,1,0:T(8,128)S(1)}, f32[1,8,64]{2,1,0:T(8,128)S(1)}, u32[]{:S(2)}, u32[]{:S(2)}) collective-permute-start(f32[1,8,64]{2,1,0:T(8,128)S(1)} %slice.176), channel_id=1, source_target_pairs={{0,8},{8,16},{16,24},{24,32},{32,40},{40,48},{48,56},{56,64},{64,7... | collective-permute-start | bytes 6152 | tf_op jit(solution)/shard_map/ppermute | solution.py:16
  67.9 63.8 %copy-start.5 = (bf16[512,64]{0,1:T(8,128)(2,1)S(1)}, bf16[512,64]{0,1:T(8,128)(2,1)}, u32[]{:S(2)}) copy-start(bf16[512,64]{0,1:T(8,128)(2,1)} %param.19) | copy-start | bytes 196612
  67.9 95.8 %copy-start.7 = (f32[64,64]{1,0:T(8,128)S(1)}, f32[64,64]{1,0:T(8,128)}, u32[]{:S(2)}) copy-start(f32[64,64]{1,0:T(8,128)} %param.23) | copy-start | bytes 49156
  70.8 63.0 %all-to-all-start = ((s32[64,1,2]{2,1,0:T(1,128)}), s32[64,1,2]{2,1,0:T(1,128)S(1)}, u32[]{:S(2)}, u32[]{:S(2)}) async-start(s32[64,1,2]{2,1,0:T(1,128)} %bitcast.2), calls=%async_computation | async-start | bytes 65536 | tf_op jit(solution)/shard_map/all_to_all | solution.py:103
  133.8 28.6 %all-to-all-start.1 = ((f32[64,1,128]{2,1,0:T(1,128)}), f32[64,1,128]{2,1,0:T(1,128)S(1)}, u32[]{:S(2)}, u32[]{:S(2)}) async-start(f32[64,1,128]{2,1,0:T(1,128)} %reshape.91), calls=%async_computation.1 | async-start | bytes 65536 | tf_op jit(solution)/shard_map/all_to_all | solution.py:102
  163.9 2.5 %copy-start.4 = (f32[64,64]{1,0:T(8,128)}, f32[64,64]{1,0:T(8,128)S(1)}, u32[]{:S(2)}) copy-start(f32[64,64]{1,0:T(8,128)S(1)} %fusion.21) | copy-start | bytes 49156
  166.5 59.0 %all-to-all-start.2 = ((f32[64,1,4096]{2,1,0:T(1,128)}), f32[64,1,4096]{2,1,0:T(1,128)S(1)}, u32[]{:S(2)}, u32[]{:S(2)}) async-start(f32[64,1,4096]{2,1,0:T(1,128)} %reshape.93), calls=%async_computation.2 | async-start | bytes 2097152 | tf_op jit(solution)/shard_map/all_to_all | solution.py:113
  228.8 4.4 %copy-start.6 = (bf16[64,512]{1,0:T(8,128)(2,1)S(1)}, bf16[64,512]{1,0:T(8,128)(2,1)}, u32[]{:S(2)}) copy-start(bf16[64,512]{1,0:T(8,128)(2,1)} %param.20) | copy-start | bytes 196612
  233.7 7.5 %collective-permute-start.9 = (f32[1,8,64]{2,1,0:T(8,128)S(1)}, f32[1,8,64]{2,1,0:T(8,128)S(1)}, u32[]{:S(2)}, u32[]{:S(2)}) collective-permute-start(f32[1,8,64]{2,1,0:T(8,128)S(1)} %slice.187), channel_id=1, source_target_pairs={{8,0},{16,8},{24,16},{32,24},{40,32},{48,40},{56,48},{64,56},{72,6... | collective-permute-start | bytes 6152 | tf_op jit(solution)/shard_map/ppermute | solution.py:19
  237.3 7.6 %collective-permute-start.8 = (f32[1,8,64]{2,1,0:T(8,128)S(1)}, f32[1,8,64]{2,1,0:T(8,128)S(1)}, u32[]{:S(2)}, u32[]{:S(2)}) collective-permute-start(f32[1,8,64]{2,1,0:T(8,128)S(1)} %slice.183), channel_id=1, source_target_pairs={{0,8},{8,16},{16,24},{24,32},{32,40},{40,48},{48,56},{56,64},{64,7... | collective-permute-start | bytes 6152 | tf_op jit(solution)/shard_map/ppermute | solution.py:16
Sparse Core Ops, SparseCore 0:
  70.2 61.4 all-reduce.1
